TPU v7x, 32 devices: a whole 2x2x4 slice. The times are simulated.
32 devices in a mesh: section: 2 (over x), dp: 16 (over z, y, core).
Axes of the slice: x: 2, y: 2, z: 4, core: 2. Of those that a mesh axis runs over, the one named last changes fastest.
Arguments:
- embeddings: bfloat16 [2, 48, 512, 512], P('section', 'dp'), may hold values from -6 to 6
- segments: int32 [2, 48, 512], P(None, 'dp'), may hold values from 0 to 23, as said below
- cotangent: bfloat16 [48, 512, 512], P('dp'), may hold values from -6 to 6
- attn_qkv: bfloat16 [2, 512, 1536], P('section'), may hold values from -0.25 to 0.25
- attn_out: bfloat16 [2, 512, 512], P('section'), may hold values from -1 to 1
- cross_proj: bfloat16 [2, 512, 1024], P('section'), may hold values from -0.375 to 0.375
- ffn_up: bfloat16 [2, 512, 2048], P('section'), may hold values from -0.25 to 0.25
- ffn_down: bfloat16 [2, 2048, 512], P('section'), may hold values from -0.125 to 0.125
- norm_gain: bfloat16 [2, 3, 512], P('section'), may hold values from 0.25 to 1.75
- norm_bias: bfloat16 [2, 3, 512], P('section'), may hold values from -1 to 1
Outputs:
- layer_out: bfloat16 [2, 48, 512, 512], P('section', 'dp')
- input_grad: float32 [2, 48, 512, 512], P('section', 'dp')
- grad_qkv: float32 [2, 512, 1536], P('section')
- grad_attn_out: float32 [2, 512, 512], P('section')
- grad_cross: float32 [2, 512, 1024], P('section')
- grad_up: float32 [2, 512, 2048], P('section')
- grad_down: float32 [2, 2048, 512], P('section')
- grad_gain: float32 [2, 3, 512], P('section')
- grad_bias: float32 [2, 3, 512], P('section')
Inputs may be any that keep to these rules, and one draw needn't show every extreme that they name: Segment numbers start at 0 in each row and rise by one at each boundary; a source row and the target row of the same index hold the same number of segments, between 8 and 24, and target segment k pairs with source segment k; some row holds 24 segments.
All inputs are finite; a program needn't handle non-finite values.
Results may differ from a plain program's by a relative error of at most 0.025.
Values may be sent and summed in bfloat16 or wider, within the bound.
A program may use at most 192 MiB of HBM per device.

v0:
```python
import jax
import jax.numpy as jnp
from jax import lax
from jax.sharding import PartitionSpec as P

HEADS = 8


epsilon = 1e-05
masked_score = -1e30


def shifted(shard, axis, by):
    size = lax.axis_size(axis)
    pairs = [(i, i + by) for i in range(size) if 0 <= i + by < size]
    return lax.ppermute(shard, axis, pairs)


def matmul(left_side, right_side):
    return jnp.dot(left_side, right_side, preferred_element_type=jnp.float32)


def left_product(left_side, right_side):
    return lax.dot_general(
        left_side, right_side, (((0,), (0,)), ((), ())), preferred_element_type=jnp.float32
    )


def right_product(left_side, right_side):
    return lax.dot_general(
        left_side, right_side, (((1,), (1,)), ((), ())), preferred_element_type=jnp.float32
    )


def normalize(values, gain_vec, bias_vec):
    center = values - jnp.mean(values, axis=-1, keepdims=True)
    spread = jnp.mean(center * center, axis=-1, keepdims=True)
    return center * lax.rsqrt(spread + epsilon) * gain_vec + bias_vec


def split_heads(values):
    return values.reshape(values.shape[0], HEADS, values.shape[1] // HEADS)


def scores_of(query_row, key_row, allowed_row):
    score_scale = (query_row.shape[1] // HEADS) ** (-0.5)
    scores = (
        jnp.einsum(
            "qhd,khd->hqk",
            split_heads(query_row),
            split_heads(key_row),
            preferred_element_type=jnp.float32,
        )
        * score_scale
    )
    return jnp.where(allowed_row[None], scores, masked_score)


def attend_rows(queries, key_rows, value_rows, allowed):

    def one_row(operands):
        query_row, key_row, value_row, allowed_row = operands
        scores = scores_of(query_row, key_row, allowed_row)
        row_top = jnp.max(scores, axis=-1, keepdims=True)
        exponent = jnp.exp(scores - row_top)
        total_mass = jnp.sum(exponent, axis=-1, keepdims=True)
        attention = (exponent / total_mass).astype(jnp.bfloat16)
        mixed_heads = jnp.einsum(
            "hqk,khd->qhd", attention, split_heads(value_row), preferred_element_type=jnp.float32
        )
        return (
            mixed_heads.reshape(query_row.shape).astype(jnp.bfloat16),
            row_top + jnp.log(total_mass),
        )

    return lax.map(one_row, (queries, key_rows, value_rows, allowed))


def attend_back(queries, key_rows, value_rows, allowed, log_mass, grad_mixed):

    def one_row(operands):
        query_row, key_row, value_row, allowed_row, mass_row, grad_row = operands
        score_scale = (query_row.shape[1] // HEADS) ** (-0.5)
        attention = jnp.exp(scores_of(query_row, key_row, allowed_row) - mass_row)
        heads_grad = split_heads(grad_row)
        grad_attention = jnp.einsum(
            "qhd,khd->hqk", heads_grad, split_heads(value_row), preferred_element_type=jnp.float32
        )
        correction = jnp.sum(grad_attention * attention, axis=-1, keepdims=True)
        grad_scores = (attention * (grad_attention - correction)).astype(jnp.bfloat16)
        grads_q = (
            jnp.einsum(
                "hqk,khd->qhd",
                grad_scores,
                split_heads(key_row),
                preferred_element_type=jnp.float32,
            )
            * score_scale
        )
        grads_k = (
            jnp.einsum(
                "hqk,qhd->khd",
                grad_scores,
                split_heads(query_row),
                preferred_element_type=jnp.float32,
            )
            * score_scale
        )
        grads_v = jnp.einsum(
            "hqk,qhd->khd",
            attention.astype(jnp.bfloat16),
            heads_grad,
            preferred_element_type=jnp.float32,
        )
        return (
            grads_q.reshape(query_row.shape),
            grads_k.reshape(key_row.shape),
            grads_v.reshape(key_row.shape),
        )

    return lax.map(one_row, (queries, key_rows, value_rows, allowed, log_mass, grad_mixed))


def self_mask(segment_ids, causal):
    allowed = segment_ids[:, :, None] == segment_ids[:, None, :]
    if causal:
        places = jnp.arange(segment_ids.shape[-1])
        allowed = allowed & (places[None, :, None] >= places[None, None, :])
    return allowed


def self_forward(low_tokens, qkv_weight, allowed, row_count):
    features = low_tokens.shape[1]
    packed = (
        matmul(low_tokens, qkv_weight).astype(jnp.bfloat16).reshape(row_count, -1, 3 * features)
    )
    mixed_heads, log_mass = attend_rows(
        packed[..., :features],
        packed[..., features : 2 * features],
        packed[..., 2 * features :],
        allowed,
    )
    return (packed, mixed_heads.reshape(-1, features), log_mass)


def self_backward(packed, allowed, log_mass, grad_mixed):
    features = packed.shape[-1] // 3
    grads_q, grads_k, grads_v = attend_back(
        packed[..., :features],
        packed[..., features : 2 * features],
        packed[..., 2 * features :],
        allowed,
        log_mass,
        grad_mixed.reshape(packed.shape[0], packed.shape[1], features),
    )
    return (
        jnp.concatenate([grads_q, grads_k, grads_v], axis=-1)
        .reshape(-1, 3 * features)
        .astype(jnp.bfloat16)
    )


def feed_forward(low_hidden, up_weight, down_weight):
    up_values = matmul(low_hidden, up_weight)
    activated = (up_values * jax.nn.sigmoid(up_values)).astype(jnp.bfloat16)
    return (matmul(activated, down_weight), up_values, activated)


def feed_backward(low_hidden, up_weight, down_weight, up_values, activated, grad_output):
    sigmoid_up = jax.nn.sigmoid(up_values)
    grad_down = left_product(activated, grad_output)
    grad_active = right_product(grad_output, down_weight)
    grad_up_values = (grad_active * (sigmoid_up * (1.0 + up_values * (1.0 - sigmoid_up)))).astype(
        jnp.bfloat16
    )
    return (
        right_product(grad_up_values, up_weight),
        left_product(low_hidden, grad_up_values),
        grad_down,
    )


def encoder_forward(weights, embed, source_ids):
    qkv_weight, out_weight, kv_weight, up_weight, down_weight, gains, biases = weights
    row_count, positions, features = embed.shape
    tokens = embed.reshape(-1, features).astype(jnp.float32)
    first_norm = normalize(tokens, gains[0], biases[0])
    packed, mixed_heads, log_mass = self_forward(
        first_norm.astype(jnp.bfloat16), qkv_weight, self_mask(source_ids, False), row_count
    )
    hidden = normalize(first_norm + matmul(mixed_heads, out_weight), gains[1], biases[1])
    branch, up_values, activated = feed_forward(hidden.astype(jnp.bfloat16), up_weight, down_weight)
    hidden = normalize(hidden + branch, gains[2], biases[2])
    low_hidden = hidden.astype(jnp.bfloat16)
    return (low_hidden, matmul(low_hidden, kv_weight).astype(jnp.bfloat16))


def encoder_backward(weights, embed, source_ids, grad_memory):
    qkv_weight, out_weight, kv_weight, up_weight, down_weight, gains, biases = weights
    row_count, positions, features = embed.shape
    tokens = embed.reshape(-1, features).astype(jnp.float32)
    first_norm, pull_first = jax.vjp(normalize, tokens, gains[0], biases[0])
    low_first = first_norm.astype(jnp.bfloat16)
    allowed = self_mask(source_ids, False)
    packed, mixed_heads, log_mass = self_forward(low_first, qkv_weight, allowed, row_count)
    hidden_one, pull_one = jax.vjp(
        normalize, first_norm + matmul(mixed_heads, out_weight), gains[1], biases[1]
    )
    low_one = hidden_one.astype(jnp.bfloat16)
    branch, up_values, activated = feed_forward(low_one, up_weight, down_weight)
    hidden_two, pull_two = jax.vjp(normalize, hidden_one + branch, gains[2], biases[2])
    low_two = hidden_two.astype(jnp.bfloat16)
    grad_kv_weight = left_product(low_two, grad_memory)
    grad_two, gain_two, bias_two = pull_two(right_product(grad_memory, kv_weight))
    grad_hidden, grad_up, grad_down = feed_backward(
        low_one, up_weight, down_weight, up_values, activated, grad_two.astype(jnp.bfloat16)
    )
    grad_one, gain_one, bias_one = pull_one(grad_two + grad_hidden)
    grad_branch = grad_one.astype(jnp.bfloat16)
    grad_out_weight = left_product(mixed_heads, grad_branch)
    grad_packed = self_backward(
        packed, allowed, log_mass, right_product(grad_branch, out_weight).astype(jnp.bfloat16)
    )
    grad_qkv_weight = left_product(low_first, grad_packed)
    grad_tokens, gain_first, bias_first = pull_first(
        grad_one + right_product(grad_packed, qkv_weight)
    )
    grads = (
        grad_qkv_weight,
        grad_out_weight,
        grad_kv_weight,
        grad_up,
        grad_down,
        jnp.stack([gain_first, gain_one, gain_two]),
        jnp.stack([bias_first, bias_one, bias_two]),
    )
    return (grad_tokens, grads)


def decoder_backward(weights, embed, target_ids, source_ids, memory_kv, cotangent):
    qkv_weight, out_weight, cross_weight, up_weight, down_weight, gains, biases = weights
    row_count, positions, features = embed.shape
    query_weight = cross_weight[:, :features]
    output_weight = cross_weight[:, features:]
    tokens = embed.reshape(-1, features).astype(jnp.float32)
    lowered = embed.reshape(-1, features)
    own_mask = self_mask(target_ids, True)
    packed, mixed_heads, log_mass = self_forward(lowered, qkv_weight, own_mask, row_count)
    hidden_one, pull_one = jax.vjp(
        normalize, tokens + matmul(mixed_heads, out_weight), gains[0], biases[0]
    )
    low_one = hidden_one.astype(jnp.bfloat16)
    queries = (
        matmul(low_one, query_weight).astype(jnp.bfloat16).reshape(row_count, positions, features)
    )
    memory_rows = memory_kv.reshape(row_count, positions, 2 * features)
    cross_mask = target_ids[:, :, None] == source_ids[:, None, :]
    cross_mixed, cross_mass = attend_rows(
        queries, memory_rows[..., :features], memory_rows[..., features:], cross_mask
    )
    cross_mixed = cross_mixed.reshape(-1, features)
    hidden_two, pull_two = jax.vjp(
        normalize, hidden_one + matmul(cross_mixed, output_weight), gains[1], biases[1]
    )
    low_two = hidden_two.astype(jnp.bfloat16)
    branch, up_values, activated = feed_forward(low_two, up_weight, down_weight)
    result, pull_three = jax.vjp(normalize, hidden_two + branch, gains[2], biases[2])
    grad_three, gain_three, bias_three = pull_three(
        cotangent.reshape(-1, features).astype(jnp.float32)
    )
    grad_hidden, grad_up, grad_down = feed_backward(
        low_two, up_weight, down_weight, up_values, activated, grad_three.astype(jnp.bfloat16)
    )
    grad_two, gain_two, bias_two = pull_two(grad_three + grad_hidden)
    grad_cross_branch = grad_two.astype(jnp.bfloat16)
    grad_output_weight = left_product(cross_mixed, grad_cross_branch)
    grad_cross_mixed = (
        right_product(grad_cross_branch, output_weight)
        .astype(jnp.bfloat16)
        .reshape(row_count, positions, features)
    )
    grads_q, grads_k, grads_v = attend_back(
        queries,
        memory_rows[..., :features],
        memory_rows[..., features:],
        cross_mask,
        cross_mass,
        grad_cross_mixed,
    )
    grad_queries = grads_q.reshape(-1, features).astype(jnp.bfloat16)
    grad_memory = (
        jnp.concatenate([grads_k, grads_v], axis=-1).reshape(-1, 2 * features).astype(jnp.bfloat16)
    )
    grad_query_weight = left_product(low_one, grad_queries)
    grad_one, gain_one, bias_one = pull_one(grad_two + right_product(grad_queries, query_weight))
    grad_branch = grad_one.astype(jnp.bfloat16)
    grad_out_weight = left_product(mixed_heads, grad_branch)
    grad_packed = self_backward(
        packed, own_mask, log_mass, right_product(grad_branch, out_weight).astype(jnp.bfloat16)
    )
    grad_qkv_weight = left_product(lowered, grad_packed)
    grad_tokens = grad_one + right_product(grad_packed, qkv_weight)
    grads = (
        grad_qkv_weight,
        grad_out_weight,
        jnp.concatenate([grad_query_weight, grad_output_weight], axis=1),
        grad_up,
        grad_down,
        jnp.stack([gain_one, gain_two, gain_three]),
        jnp.stack([bias_one, bias_two, bias_three]),
    )
    return (result.astype(jnp.bfloat16), grad_tokens, grad_memory, grads)


def per_device(
    embeddings,
    segments,
    cotangent,
    attn_qkv,
    attn_out,
    cross_proj,
    ffn_up,
    ffn_down,
    norm_gain,
    norm_bias,
):
    is_encoder = lax.axis_index("section") == 0
    weights = (
        attn_qkv[0],
        attn_out[0],
        cross_proj[0],
        ffn_up[0],
        ffn_down[0],
        norm_gain[0].astype(jnp.float32),
        norm_bias[0].astype(jnp.float32),
    )
    embed = embeddings[0]
    row_total, positions, features = embed.shape
    zero_grads = tuple((jnp.zeros(member.shape, jnp.float32) for member in weights))
    pieces = 1
    per_piece = row_total // pieces
    token_count = per_piece * positions
    piece_index = 0
    first_row = piece_index * per_piece

    def active():
        return encoder_forward(weights, embed, segments[0, first_row : first_row + per_piece])

    def resting():
        return (
            jnp.zeros((token_count, features), jnp.bfloat16),
            jnp.zeros((token_count, 2 * features), jnp.bfloat16),
        )

    memory, memory_kv = lax.cond(is_encoder, active, resting)
    memories = [memory]
    received_list = [shifted(memory_kv, "section", 1)]
    grand_total = zero_grads
    piece_index = 0
    decode_first_row = piece_index * per_piece
    received = received_list[piece_index]

    def active():
        return decoder_backward(
            weights,
            embed,
            segments[1, decode_first_row : decode_first_row + per_piece],
            segments[0, decode_first_row : decode_first_row + per_piece],
            received,
            cotangent,
        )

    def resting():
        return (
            jnp.zeros((token_count, features), jnp.bfloat16),
            jnp.zeros((token_count, features), jnp.float32),
            jnp.zeros((token_count, 2 * features), jnp.bfloat16),
            zero_grads,
        )

    result, decoder_tokens, grad_memory, decoder_grads = lax.cond(is_encoder, resting, active)
    returned = shifted(grad_memory, "section", -1)
    encode_first_row = piece_index * per_piece

    def active():
        return encoder_backward(
            weights, embed, segments[0, encode_first_row : encode_first_row + per_piece], returned
        )

    def resting():
        return (jnp.zeros((token_count, features), jnp.float32), zero_grads)

    encoder_tokens, encoder_grads = lax.cond(is_encoder, active, resting)
    block_sum = tuple(
        (
            jnp.add(first_term, second_term)
            for first_term, second_term in zip(decoder_grads, encoder_grads)
        )
    )
    grand_total = tuple(
        (
            jnp.add(first_term, second_term)
            for first_term, second_term in zip(grand_total, block_sum)
        )
    )
    results = jnp.where(is_encoder, memories[piece_index], result)
    token_grads = decoder_tokens + encoder_tokens
    grand_total = lax.psum(grand_total, "dp")
    layer_out = results.reshape(1, row_total, positions, features)
    input_grad = token_grads.reshape(1, row_total, positions, features)
    return (
        layer_out,
        input_grad,
        grand_total[0][None],
        grand_total[1][None],
        grand_total[2][None],
        grand_total[3][None],
        grand_total[4][None],
        grand_total[5][None],
        grand_total[6][None],
    )


def solution(mesh):
    in_specs = (
        P("section", "dp", None, None),
        P(None, "dp", None),
        P("dp", None, None),
        P("section", None, None),
        P("section", None, None),
        P("section", None, None),
        P("section", None, None),
        P("section", None, None),
        P("section", None, None),
        P("section", None, None),
    )
    out_specs = (
        P("section", "dp", None, None),
        P("section", "dp", None, None),
        P("section", None, None),
        P("section", None, None),
        P("section", None, None),
        P("section", None, None),
        P("section", None, None),
        P("section", None, None),
        P("section", None, None),
    )
    return jax.shard_map(
        per_device, mesh=mesh, in_specs=in_specs, out_specs=out_specs, check_vma=False
    )
```

profile of v0, /device:TPU:0, one launch (start us, length us, event | category | flops | bytes accessed | tf_op | source)
XLA Modules:
  0.0 1111.2 jit_solution(4176802857743177731)
XLA Ops:
  7.9 85.9 %conditional.3 = (bf16[1536,512]{0,1:T(8,128)(2,1)}, bf16[1536,1024]{1,0:T(8,128)(2,1)}) conditional(s32[]{:T(128)} %convert_element_type.252, () %tuple.60, (bf16[1,3,512,512]{3,2,1,0:T(8,128)(2,1)}, f32[3,512]{1,0:T(4,128)S(1)}, f32[3,512]{1,0:T(4,128)S(1)}, bf16[512,1536]{1,0:T(8,128)(2,1)}, s32[2,3,512]{2,0,1:T(2,128)}, ...), branch_computations={%region_0.0_spmd, %region_1.12_spmd} | conditional | flops 11875128320 | bytes 133538168 | solution.py:355
  9.8 2.1 multiply_reduce_fusion.2
  13.3 2.1 copy.64
  15.4 5.3 convolution_convert_fusion
  20.7 2.0 fusion.126
  22.7 44.9 %while.87 = (s32[]{:T(128)}, bf16[3,512,512]{2,1,0:T(8,128)(2,1)}, bf16[3,512,512]{2,1,0:T(8,128)(2,1)}, pred[3,512,512]{1,2,0:T(8,128)(4,1)}, bf16[3,512,512]{2...) while((s32[]{:T(128)}, bf16[3,512,512]{2,1,0:T(8,128)(2,1)}, bf16[3,512,512]{2,1,0:T(8,128)(2,1)}, ...), condition=%wide.region_7.7_spmd, body=%wide.region_4.6_spmd.sunk | while | flops 549716480 | bytes 40665244 | solution.py:76
  26.7 5.4 fusion.355
  32.2 4.3 fusion.356
  41.6 5.4 fusion.355
  47.0 4.3 fusion.356
  56.4 5.4 fusion.355
  61.8 4.3 fusion.356
  67.7 3.9 fusion.129
  73.3 13.4 %fusion.130 = (f32[1536]{0:T(1024)S(1)}, f32[1536,512]{0,1:T(8,128)S(1)}) fusion(bf16[2048,512]{1,0:T(8,128)(2,1)} %get-tuple-element.303, bf16[512,2048]{1,0:T(8,128)(2,1)} %get-tuple-element.302, f32[1536,512]{0,1:T(8,128)} %copy-done.32, f32[512]{0:T(512)S(1)} %bitcast.595, f32[512]{0:T(512)S(1)} %bitcast.594, f32[1536]{0:T(1024)S(1)} %add_rsqrt_fusion.1, ...), kind=kOutput, calls=%fused_computation.317 | convolution fusion | flops 6466828800 | bytes 10508288 | tf_op jit(solution)/shard_map/cond/branch_1_fun/dot_general | solution.py:20
  88.8 4.9 convolution_convert_fusion.1
  95.4 68.3 %collective-permute-done = bf16[1536,1024]{1,0:T(8,128)(2,1)S(1)} collective-permute-done((bf16[1536,1024]{1,0:T(8,128)(2,1)}, bf16[1536,1024]{1,0:T(8,128)(2,1)S(1)}, u32[]{:S(2)}, u32[]{:S(2)}) %collective-permute-start) | collective-permute-done | bytes 3145760 | tf_op jit(solution)/shard_map/ppermute | solution.py:16
  163.7 18.3 %conditional.4 = (bf16[1536,512]{0,1:T(8,128)(2,1)}, bf16[1536,1024]{1,0:T(8,128)(2,1)}, f32[512,512]{1,0:T(8,128)}, f32[512,2048]{1,0:T(8,128)}, f32[2048,512]{...) conditional(s32[]{:T(128)} %convert_element_type.252, ...), branch_computations={%region_12.45_spmd, %region_45.46_spmd} | conditional | flops 37867507712 | bytes 836867840 | solution.py:381
  172.4 2.1 broadcast.406
  174.8 2.1 broadcast.405.clone
  176.9 2.5 broadcast_in_dim.208
  179.5 2.5 broadcast_in_dim.207
  183.3 416.6 %collective-permute-done.1 = bf16[1536,1024]{1,0:T(8,128)(2,1)} collective-permute-done((bf16[1536,1024]{1,0:T(8,128)(2,1)}, bf16[1536,1024]{1,0:T(8,128)(2,1)}, u32[]{:S(2)}, u32[]{:S(2)}) %collective-permute-start.1) | collective-permute-done | bytes 3145760 | tf_op jit(solution)/shard_map/ppermute | solution.py:16
  599.9 199.4 %conditional.5 = (f32[1536,512]{1,0:T(8,128)}, f32[512,1536]{1,0:T(8,128)}, f32[512,512]{1,0:T(8,128)S(1)}, f32[512,1024]{1,0:T(8,128)}, f32[512,2048]{1,0:T(8,1...) conditional(s32[]{:T(128)} %convert_element_type.252, () %tuple.64, ...), branch_computations={%region_46.47_spmd, %region_47.73_spmd} | conditional | flops 34315198464 | bytes 580767040 | solution.py:393
  601.8 2.1 multiply_reduce_fusion.23
  608.6 3.3 convolution_convert_fusion.6
  613.4 2.6 copy.195
  619.2 28.2 %while.85 = (s32[]{:T(128)}, bf16[3,512,512]{2,1,0:T(8,128)(2,1)S(1)}, f32[3,8,512,1]{2,1,3,0:T(8,128)S(1)}, bf16[3,512,512]{1,2,0:T(8,128)(2,1)}, pred[3,512,51...) while((s32[]{:T(128)}, ...), condition=%wide.region_53.53_spmd, body=%wide.region_50.52_spmd.sunk | while | flops 562294784 | bytes 33947760 | solution.py:76
  625.8 2.5 fusion.303
  635.2 2.5 fusion.303
  644.6 2.5 fusion.303
  647.4 3.0 fusion.143
  652.0 7.7 multiply_convert_fusion.10
  659.8 4.2 fusion.144
  664.6 5.4 fusion.102
  670.0 5.3 multiply_reduce_fusion.15
  677.0 8.3 multiply_convert_fusion.9
  685.3 8.8 fusion.112
  694.1 4.9 multiply_reduce_fusion.16
  699.0 5.4 fusion.115
  708.1 2.2 convolution_convert_fusion.7
  710.3 70.0 %while.86 = (s32[]{:T(128)}, bf16[3,512,512]{2,1,0:T(8,128)(2,1)}, bf16[3,512,512]{2,1,0:T(8,128)(2,1)}, bf16[3,512,512]{2,1,0:T(8,128)(2,1)}, bf16[3,512,512]{1...) while((s32[]{:T(128)}, bf16[3,512,512]{2,1,0:T(8,128)(2,1)}, ...), condition=%wide.region_64.64_spmd, body=%wide.region_62.63_spmd.sunk | while | flops 1374679040 | bytes 148226256 | solution.py:121
  717.4 2.3 fusion.315
  720.9 5.1 multiply_reduce_fusion.27
  726.7 2.6 multiply_convert_fusion.14
  740.7 2.3 fusion.315
  744.1 5.1 multiply_reduce_fusion.27
  749.9 2.6 multiply_convert_fusion.14
  764.0 2.3 fusion.315
  767.4 5.1 multiply_reduce_fusion.27
  773.2 2.6 multiply_convert_fusion.14
  780.4 7.3 fusion.95
  790.6 3.6 fusion.119
  796.1 3.0 broadcast_add_fusion
  800.2 6.7 add_bitcast_fusion
  806.9 5.1 add_bitcast_fusion.1
  812.0 3.4 add_bitcast_fusion.3
  817.8 4.2 add_bitcast_fusion.2
  822.0 2.9 broadcast_select_fusion
  824.9 2.6 copy.117
  827.6 5.0 add.341
  832.6 63.6 %all-reduce = (f32[1,3,512]{2,0,1:T(1,128)}, f32[1,3,512]{2,0,1:T(1,128)}) all-reduce(f32[1,3,512]{2,0,1:T(1,128)S(1)} %broadcast_in_dim.241, f32[1,3,512]{2,0,1:T(1,128)S(1)} %broadcast_in_dim.242), channel_id=1, replica_groups=mesh['section'=2,'dp'=16] {'dp'}, use_global_device_ids=true, to_apply=%region_78.79 | all-reduce | flops 3072 | bytes 24576 | tf_op jit(solution)/shard_map/psum | solution.py:408
  896.2 195.1 %all-reduce.4.cloned.1.call-done = (f32[1,512,1536]{2,1,0:T(8,128)}, f32[1,512,512]{2,1,0:T(8,128)}, f32[1,512,1024]{2,1,0:T(8,128)}, f32[1,512,2048]{2,1,0:T(8,128)}, f32[1,2048,512]{2,1,0:T(8,128)}) async-done(((f32[1,512,1536]{2,1,0:T(8,128)}, f32[1,512,512]{2,1,0:T(8,128)}, f32[1,512,1024]{2,1,0:T(8,128)}, f32[1,512,2048]{2,1,0:T(8,128)}, f32[1,2048,512]{2,1,0:T(8,128)}), (f32[1,512,1536]{2,1,0:T(8,128)}, ...) | async-done | bytes 14680080 | tf_op jit(solution)/shard_map/psum | solution.py:408
  1091.2 3.9 copy.389
  1098.5 2.1 copy.392
  (302 shorter events, 123.5 us)
Async XLA Ops:
  7.2 1084.1 %all-reduce.4.cloned.1.call-start = ((), (), s32[]{:S(2)}) async-start(), calls=%async_computation | async-start | bytes 29360128 | tf_op jit(solution)/shard_map/psum | solution.py:408
  7.9 155.8 %copy-start.63 = (f32[3,512]{1,0:T(4,128)}, f32[3,512]{1,0:T(4,128)S(1)}, u32[]{:S(2)}) copy-start(f32[3,512]{1,0:T(4,128)S(1)} %get-tuple-element.831) | copy-start | bytes 18436
  7.9 4.0 copy-start.60
  7.9 5.4 copy-start.4
  11.9 3.5 copy-start.93
  22.7 3.6 copy-start.19
  32.2 5.4 copy-start.20
  37.6 3.6 copy-start.19
  47.0 5.4 copy-start.20
  52.4 3.6 copy-start.19
  61.8 5.4 copy-start.20
  87.1 1.7 copy-start.48
  93.9 69.8 %collective-permute-start = (bf16[1536,1024]{1,0:T(8,128)(2,1)}, bf16[1536,1024]{1,0:T(8,128)(2,1)S(1)}, u32[]{:S(2)}, u32[]{:S(2)}) collective-permute-start(bf16[1536,1024]{1,0:T(8,128)(2,1)} %get-tuple-element.428), channel_id=1, source_target_pairs={{0,16},{1,17},{2,18},{3,19},{4,20},{5,21},{6,22},{7,23},{8,24},{9,... | collective-permute-start | bytes 9437192 | tf_op jit(solution)/shard_map/ppermute | solution.py:16
  182.0 417.9 %copy-start.15 = (f32[512,1536]{1,0:T(8,128)}, f32[512,1536]{1,0:T(8,128)S(1)}, u32[]{:S(2)}) copy-start(f32[512,1536]{1,0:T(8,128)S(1)} %get-tuple-element.584) | copy-start | bytes 9437188
  182.0 417.9 %copy-start.71 = (f32[3,512]{1,0:T(4,128)}, f32[3,512]{1,0:T(4,128)S(1)}, u32[]{:S(2)}) copy-start(f32[3,512]{1,0:T(4,128)S(1)} %get-tuple-element.443) | copy-start | bytes 18436
  182.0 417.9 %copy-start.73 = (f32[3,512]{1,0:T(4,128)}, f32[3,512]{1,0:T(4,128)S(1)}, u32[]{:S(2)}) copy-start(f32[3,512]{1,0:T(4,128)S(1)} %get-tuple-element.445) | copy-start | bytes 18436
  182.0 417.9 %collective-permute-start.1 = (bf16[1536,1024]{1,0:T(8,128)(2,1)}, bf16[1536,1024]{1,0:T(8,128)(2,1)}, u32[]{:S(2)}, u32[]{:S(2)}) collective-permute-start(bf16[1536,1024]{1,0:T(8,128)(2,1)} %get-tuple-element.431), channel_id=1, source_target_pairs={{16,0},{17,1},{18,2},{19,3},{20,4},{21,5},{22,6},{23,7},{24,8},{25... | collective-permute-start | bytes 9437192 | tf_op jit(solution)/shard_map/ppermute | solution.py:16
  599.9 4.0 copy-start.64
  599.9 4.1 copy-start.62
  599.9 5.5 copy-start.7
  601.8 6.0 copy-start.54
  603.9 3.9 copy-start.67
  603.9 3.9 copy-start.56
  603.9 3.9 copy-start.69
  608.6 3.3 copy-start.14
  619.2 28.3 %copy-start.38 = (bf16[512,512]{1,0:T(8,128)(2,1)S(1)}, bf16[512,512]{1,0:T(8,128)(2,1)}, u32[]{:S(2)}) copy-start(bf16[512,512]{1,0:T(8,128)(2,1)} %get-tuple-element.391) | copy-start | bytes 1572868 | tf_op jit(solution)/shard_map/cond
  652.0 7.8 copy-start.92
  659.8 4.2 copy-start.97
  664.6 5.4 copy-start.51
  706.0 2.1 copy-start.35
  717.4 3.2 copy-start.2
  720.9 5.8 copy-start.3
  740.7 3.2 copy-start.2
  744.1 5.8 copy-start.3
  763.9 3.2 copy-start.2
  767.4 5.8 copy-start.3
  780.4 7.3 copy-start.39
  780.4 7.3 copy-start.40
  780.4 7.3 copy-start.41
  787.7 2.4 copy-start.36
  787.7 2.3 copy-start.55
  787.7 2.3 copy-start.70
  787.7 2.8 copy-start.96
  790.5 3.6 copy-start.68
  790.5 3.6 copy-start.88
  790.6 3.6 copy-start.57
  794.1 1.9 copy-start.87
  796.1 3.0 copy-start.26
  799.3 7.6 copy-start.75
  799.3 7.6 copy-start.77
  800.2 6.7 copy-start.25
  806.9 5.1 copy-start.21
  812.0 3.5 copy-start.28
  812.0 3.5 copy-start.45
  815.5 2.3 copy-start.16
  822.0 5.5 copy-start.74
  822.0 5.5 copy-start.76
  822.0 5.5 copy-start.72
  822.0 5.5 copy-start.78
  822.0 5.6 copy-start.17
  1091.2 3.9 copy-start.46
  1091.2 4.9 copy-start.37
  1095.2 3.3 copy-start.30
  1098.5 3.7 copy-start.29
  (6 other events, 8.6 us)
Sparse Core Ops, SparseCore 0:
  822.1 269.0 all-reduce.3
where the time goes:
time: 1120 us; the launch traced here: 1110 us
  waiting for transfers between devices  680 us (61%)
  matrix products  173 us (15%)
  local copies, waits for them, and re-layouts  102 us (9%)
  other arithmetic  68.1 us (6%)
  blocking collectives  63.6 us (6%)
  between operations  14.4 us (1%)
    ppermute x2, waiting for transfers between devices, shifted(): return lax.ppermute(shard, axis, pairs)  485 us
    psum x1, waiting for transfers between devices, per_device(): grand_total = lax.psum(grand_total, 'dp')  195 us
    psum x1, blocking collectives, per_device(): grand_total = lax.psum(grand_total, 'dp')  63.6 us
    dot_general x8, matrix products, matmul(): return jnp.dot(left_side, right_side, preferred_element_type=jnp.float32)  45.7 us
    dynamic_slice x36, local copies, waits for them, and re-layouts, attend_rows(): return lax.map(one_row, (queries, key_rows, value_rows, allowed))  29.2 us
    dot_general x5, matrix products, left_product(): lax.dot_general(left_side, right_side, (((0,), (0,)), ((), ())), preferre...  28.9 us
    dot_general x5, matrix products, right_product(): lax.dot_general(left_side, right_side, (((1,), (1,)), ((), ())), preferre...  24.2 us
  transfers between devices with their start and end apart: 3, of which 3 were waited for; matrix products, arithmetic and copies ran while one was open for 1% of the time, Pallas kernels for 0%

commit v1 on v0

--- a/solution.py
+++ b/solution.py
@@ -2,6 +2,179 @@
 import jax.numpy as jnp
 from jax import lax
 from jax.sharding import PartitionSpec as P
+import functools
+from jax.experimental import pallas as pl
+from jax.experimental.pallas import tpu as pltpu
+
+bf16, f32 = jnp.bfloat16, jnp.float32
+PARTS = 3
+
+def ring_place(index, chips):
+    chip = lax.div(index, 2)
+    level, side = lax.div(chip, 2), lax.rem(chip, 2)
+    return jnp.where(side == 0, level, chips - 1 - level)
+
+def ring_device(place, chips, core):
+    half = chips // 2
+    chip = jnp.where(place < half, 2 * place, 2 * (chips - 1 - place) + 1)
+    return 2 * chip + core
+
+def sum_kernel(chips, local, total, paired, landed, pair_sems, ring_sems, gather_sems, share_sems):
+    width = local.shape[1]
+    part = width // PARTS
+    me = lax.axis_index("dp")
+    core = lax.rem(me, 2)
+    place = ring_place(me, chips)
+    sibling = me + 1 - 2 * core
+    ahead = ring_device(lax.rem(place + 1, chips), chips, core)
+    behind = ring_device(lax.rem(place + chips - 1, chips), chips, core)
+    targets = (ahead, behind)
+
+    barrier = pltpu.get_barrier_semaphore()
+    for other in (sibling, ahead, behind):
+        pl.semaphore_signal(barrier, inc=1, device_id={"dp": other}, device_id_type=pl.DeviceIdType.MESH)
+    pl.semaphore_wait(barrier, 3)
+
+    def slot(way, step):
+        return lax.rem(place + (chips - step if way == 0 else step), chips)
+
+    def rows(way, step, owner):
+        return pl.ds(pl.multiple_of(64 * slot(way, step) + 32 * owner + 16 * way, 16), 16)
+
+    def pair_copy(way, step):
+        return pltpu.make_async_remote_copy(
+            src_ref=local.at[rows(way, step, 1 - core)],
+            dst_ref=paired.at[way, step],
+            send_sem=pair_sems.at[0, way, step],
+            recv_sem=pair_sems.at[1, way, step],
+            device_id={"dp": sibling}, device_id_type=pl.DeviceIdType.MESH)
+
+    def columns(p):
+        return pl.ds(p * part, part)
+
+    def ring_copy(way, step, p):
+        return pltpu.make_async_remote_copy(
+            src_ref=paired.at[way, step, :, columns(p)],
+            dst_ref=landed.at[way, step, :, columns(p)],
+            send_sem=ring_sems.at[0, way, step, p],
+            recv_sem=ring_sems.at[1, way, step, p],
+            device_id={"dp": targets[way]}, device_id_type=pl.DeviceIdType.MESH)
+
+    def gather_copy(way, step, p):
+        span = rows_gather(way, step)
+        return pltpu.make_async_remote_copy(
+            src_ref=total.at[span, columns(p)],
+            dst_ref=total.at[span, columns(p)],
+            send_sem=gather_sems.at[0, way, step, p],
+            recv_sem=gather_sems.at[1, way, step, p],
+            device_id={"dp": targets[way]}, device_id_type=pl.DeviceIdType.MESH)
+
+    def rows_gather(way, step):
+        shift = lax.rem(chips - 1 + step, chips)
+        place_of = lax.rem(place + (chips - shift if way == 0 else shift), chips)
+        return pl.ds(pl.multiple_of(64 * place_of + 32 * core + 16 * way, 16), 16)
+
+    def share_copy(way, step):
+        span = rows_gather(way, step)
+        return pltpu.make_async_remote_copy(
+            src_ref=total.at[span],
+            dst_ref=total.at[span],
+            send_sem=share_sems.at[0, way, step],
+            recv_sem=share_sems.at[1, way, step],
+            device_id={"dp": sibling}, device_id_type=pl.DeviceIdType.MESH)
+
+    def pair_start(step, carry):
+        for way in range(2):
+            pair_copy(way, step).start()
+        return carry
+    lax.fori_loop(0, chips, pair_start, 0)
+
+    for way in range(2):
+        pair_copy(way, 0).wait_recv()
+        for p in range(PARTS):
+            mine = local[rows(way, 0, core), p * part:(p + 1) * part].astype(f32)
+            paired[way, 0, :, p * part:(p + 1) * part] = (mine + paired[way, 0, :, p * part:(p + 1) * part].astype(f32)).astype(bf16)
+            ring_copy(way, 0, p).start()
+
+    def reduce_step(step, carry):
+        for way in range(2):
+            pair_copy(way, step).wait_recv()
+        for p in range(PARTS):
+            for way in range(2):
+                ring_copy(way, step - 1, p).wait_recv()
+                cols = slice(p * part, (p + 1) * part)
+                mine = local[rows(way, step, core), cols].astype(f32)
+                paired[way, step, :, cols] = (
+                    mine + paired[way, step, :, cols].astype(f32) + landed[way, step - 1, :, cols].astype(f32)
+                ).astype(bf16)
+                ring_copy(way, step, p).start()
+        return carry
+    lax.fori_loop(1, chips - 1, reduce_step, 0)
+
+    last = chips - 1
+    for way in range(2):
+        pair_copy(way, last).wait_recv()
+    for p in range(PARTS):
+        for way in range(2):
+            ring_copy(way, last - 1, p).wait_recv()
+            cols = slice(p * part, (p + 1) * part)
+            mine = local[rows(way, last, core), cols].astype(f32)
+            total[rows(way, last, core), cols] = (
+                mine + paired[way, last, :, cols].astype(f32) + landed[way, last - 1, :, cols].astype(f32)
+            ).astype(bf16)
+            gather_copy(way, 0, p).start()
+    for way in range(2):
+        share_copy(way, 0).start()
+
+    def gather_step(step, carry):
+        for p in range(PARTS):
+            for way in range(2):
+                gather_copy(way, step - 1, p).wait_recv()
+                gather_copy(way, step, p).start()
+        for way in range(2):
+            share_copy(way, step).start()
+        return carry
+    lax.fori_loop(1, chips - 1, gather_step, 0)
+    for p in range(PARTS):
+        for way in range(2):
+            gather_copy(way, last - 1, p).wait_recv()
+    for way in range(2):
+        share_copy(way, last).start()
+
+    def finish(step, carry):
+        for way in range(2):
+            pair_copy(way, step).wait_send()
+            share_copy(way, step).wait()
+        return carry
+    lax.fori_loop(0, chips, finish, 0)
+
+    def finish_ring(step, carry):
+        for way in range(2):
+            for p in range(PARTS):
+                ring_copy(way, step, p).wait_send()
+                gather_copy(way, step, p).wait_send()
+        return carry
+    lax.fori_loop(0, chips - 1, finish_ring, 0)
+
+
+def sum_over(local, devices):
+    chips = devices // 2
+    width = local.shape[1]
+    return pl.pallas_call(
+        functools.partial(sum_kernel, chips),
+        out_shape=jax.ShapeDtypeStruct(local.shape, bf16),
+        in_specs=[pl.BlockSpec(memory_space=pltpu.VMEM)],
+        out_specs=pl.BlockSpec(memory_space=pltpu.VMEM),
+        scratch_shapes=[
+            pltpu.VMEM((2, chips, 16, width), bf16),
+            pltpu.VMEM((2, chips - 1, 16, width), bf16),
+            pltpu.SemaphoreType.DMA((2, 2, chips)),
+            pltpu.SemaphoreType.DMA((2, 2, chips - 1, PARTS)),
+            pltpu.SemaphoreType.DMA((2, 2, chips - 1, PARTS)),
+            pltpu.SemaphoreType.DMA((2, 2, chips)),
+        ],
+        compiler_params=pltpu.CompilerParams(collective_id=0, has_side_effects=True, vmem_limit_bytes=60 << 20),
+    )(local)
 
 HEADS = 8
 
@@ -405,7 +578,7 @@
     )
     results = jnp.where(is_encoder, memories[piece_index], result)
     token_grads = decoder_tokens + encoder_tokens
-    grand_total = lax.psum(grand_total, "dp")
+    grand_total = sum_gradients(grand_total)
     layer_out = results.reshape(1, row_total, positions, features)
     input_grad = token_grads.reshape(1, row_total, positions, features)
     return (
@@ -421,6 +594,35 @@
     )
 
 
+def sum_gradients(grads):
+    qkv, out, cross, up, down, gain, bias = grads
+    features, hidden = up.shape
+    devices = lax.axis_size("dp")
+    blocks = hidden // features
+    norms = jnp.concatenate([gain, bias]).T
+    norms = jnp.pad(norms, ((0, 0), (0, 128 - norms.shape[1])))
+    packed = jnp.concatenate(
+        [qkv, out, cross, up]
+        + [down[i * features : (i + 1) * features] for i in range(blocks)]
+        + [norms],
+        axis=1,
+    ).astype(bf16)
+    if features == 32 * devices:
+        packed = sum_over(packed, devices)
+    else:
+        packed = lax.psum(packed, "dp")
+    packed = packed.astype(f32)
+    pieces, start = [], 0
+    for member in (qkv, out, cross, up):
+        pieces.append(packed[:, start : start + member.shape[1]])
+        start += member.shape[1]
+    down = jnp.concatenate(
+        [packed[:, start + i * features : start + (i + 1) * features] for i in range(blocks)]
+    )
+    norms = packed[:, start + blocks * features :]
+    return (*pieces, down, norms[:, :3].T, norms[:, 3:6].T)
+
+
 def solution(mesh):
     in_specs = (
         P("section", "dp", None, None),

time: 1120 us -> 950 us (0.85)
  waiting for transfers between devices: 680 us -> 485 us
  Pallas kernels: 0 us -> 84.7 us
  blocking collectives: 63.6 us -> 0 us
  between operations: 14.4 us -> 1.28 us
  local copies, waits for them, and re-layouts: 102 us -> 115 us
    psum x1 -> x0, waiting for transfers between devices: 195 us -> none  [per_device(): grand_total = lax.psum(grand_total, 'dp')]
    pallas_call x0 -> x1, Pallas kernels: none -> 84.7 us  [sum_over(): pl.pallas_call(functools.partial(sum_kernel, chips), out_shape=jax.ShapeD...]
    psum x1 -> x0, blocking collectives: 63.6 us -> none  [per_device(): grand_total = lax.psum(grand_total, 'dp')]
    broadcast_in_dim x1 -> x4, local copies, waits for them, and re-layouts: 0.01 us -> 14 us  [the longest x1 4.85 us: per_device(): grand_total[3][None]]
    broadcast_in_dim x4 -> x0, other arithmetic: 14 us -> none  [the longest x1 5.11 us: per_device(): grand_total[3][None]]
    unnamed x0 -> x4, other arithmetic: none -> 13.1 us
  transfers between devices with their start and end apart: 3 -> 2, of which waited for: 3 -> 2; matrix products, arithmetic and copies ran while one was open for 1% -> 0% of each run, Pallas kernels for 0% -> 0%
where the time goes in v1:
time: 950 us; the launch traced here: 940 us
  waiting for transfers between devices  485 us (51%)
  matrix products  175 us (18%)
  local copies, waits for them, and re-layouts  115 us (12%)
  Pallas kernels  84.7 us (9%)
  other arithmetic  68.8 us (7%)
    ppermute x2, waiting for transfers between devices, shifted(): return lax.ppermute(shard, axis, pairs)  485 us
    pallas_call x1, Pallas kernels, sum_over(): pl.pallas_call(functools.partial(sum_kernel, chips), out_shape=jax.ShapeD...  84.7 us
    dot_general x8, matrix products, matmul(): return jnp.dot(left_side, right_side, preferred_element_type=jnp.float32)  48.1 us
    dynamic_slice x36, local copies, waits for them, and re-layouts, attend_rows(): return lax.map(one_row, (queries, key_rows, value_rows, allowed))  29.2 us
    dot_general x5, matrix products, left_product(): lax.dot_general(left_side, right_side, (((0,), (0,)), ((), ())), preferre...  29 us
    dot_general x5, matrix products, right_product(): lax.dot_general(left_side, right_side, (((1,), (1,)), ((), ())), preferre...  24.2 us
    dot_general x6, matrix products, one_row(): jnp.einsum('hqk,khd->qhd', attention, split_heads(value_row), preferred_e...  20.6 us
  transfers between devices with their start and end apart: 2, of which 2 were waited for; matrix products, arithmetic and copies ran while one was open for 0% of the time, Pallas kernels for 0%

profile of v1, /device:TPU:0, one launch (start us, length us, event | category | flops | bytes accessed | tf_op | source)
XLA Modules:
  0.0 940.3 jit_solution(1084506108065229121)
XLA Ops:
  1.4 85.7 %conditional.3 = (bf16[1536,512]{0,1:T(8,128)(2,1)}, bf16[1536,1024]{1,0:T(8,128)(2,1)}) conditional(s32[]{:T(128)} %convert_element_type.258, () %tuple.60, (bf16[1,3,512,512]{3,2,1,0:T(8,128)(2,1)}, f32[3,512]{1,0:T(4,128)S(1)}, f32[3,512]{1,0:T(4,128)S(1)}, bf16[512,1536]{1,0:T(8,128)(2,1)}, s32[2,3,512]{2,0,1:T(2,128)}, ...), branch_computations={%region_0.0_spmd, %region_1.12_spmd} | conditional | flops 11875128320 | bytes 133538168 | solution.py:528
  3.2 2.1 multiply_reduce_fusion.2
  8.8 5.3 convolution_convert_fusion
  16.1 44.7 %while.87 = (s32[]{:T(128)}, bf16[3,512,512]{2,1,0:T(8,128)(2,1)}, bf16[3,512,512]{2,1,0:T(8,128)(2,1)}, pred[3,512,512]{1,2,0:T(8,128)(4,1)}, bf16[3,512,512]{2...) while((s32[]{:T(128)}, bf16[3,512,512]{2,1,0:T(8,128)(2,1)}, bf16[3,512,512]{2,1,0:T(8,128)(2,1)}, ...), condition=%wide.region_7.7_spmd, body=%wide.region_4.6_spmd.sunk | while | flops 549716480 | bytes 40665244 | solution.py:249
  20.2 5.4 fusion.360
  25.6 4.3 fusion.361
  35.0 5.4 fusion.360
  40.4 4.3 fusion.361
  49.9 5.4 fusion.360
  55.3 4.3 fusion.361
  60.8 3.9 fusion.133
  66.4 13.4 %fusion.134 = (f32[1536]{0:T(1024)S(1)}, f32[1536,512]{0,1:T(8,128)S(1)}) fusion(bf16[2048,512]{1,0:T(8,128)(2,1)} %get-tuple-element.303, bf16[512,2048]{1,0:T(8,128)(2,1)} %get-tuple-element.302, f32[1536,512]{0,1:T(8,128)} %copy-done.33, f32[512]{0:T(512)S(1)} %bitcast.605, f32[512]{0:T(512)S(1)} %bitcast.604, f32[1536]{0:T(1024)S(1)} %add_rsqrt_fusion.1, ...), kind=kOutput, calls=%fused_computation.336 | convolution fusion | flops 6466828800 | bytes 10508288 | tf_op jit(solution)/shard_map/cond/branch_1_fun/dot_general | solution.py:193
  82.0 4.9 convolution_convert_fusion.1
  88.6 68.4 %collective-permute-done = bf16[1536,1024]{1,0:T(8,128)(2,1)S(1)} collective-permute-done((bf16[1536,1024]{1,0:T(8,128)(2,1)}, bf16[1536,1024]{1,0:T(8,128)(2,1)S(1)}, u32[]{:S(2)}, u32[]{:S(2)}) %collective-permute-start) | collective-permute-done | bytes 3145760 | tf_op jit(solution)/shard_map/ppermute | solution.py:189
  156.9 18.8 %conditional.4 = (bf16[1536,512]{0,1:T(8,128)(2,1)}, bf16[1536,1024]{1,0:T(8,128)(2,1)}, f32[512,512]{1,0:T(8,128)}, f32[512,2048]{1,0:T(8,128)}, f32[2048,512]{...) conditional(s32[]{:T(128)} %convert_element_type.258, ...), branch_computations={%region_12.45_spmd, %region_45.46_spmd} | conditional | flops 37867507712 | bytes 836867840 | solution.py:554
  168.6 2.1 broadcast.405.clone
  170.7 2.5 broadcast_in_dim.208
  173.2 2.5 broadcast_in_dim.207
  180.7 417.1 %collective-permute-done.1 = bf16[1536,1024]{1,0:T(8,128)(2,1)} collective-permute-done((bf16[1536,1024]{1,0:T(8,128)(2,1)}, bf16[1536,1024]{1,0:T(8,128)(2,1)}, u32[]{:S(2)}, u32[]{:S(2)}) %collective-permute-start.1) | collective-permute-done | bytes 3145760 | tf_op jit(solution)/shard_map/ppermute | solution.py:189
  597.9 198.3 %conditional.5 = (f32[1536,512]{1,0:T(8,128)}, f32[512,1536]{1,0:T(8,128)}, f32[512,512]{1,0:T(8,128)}, f32[512,1024]{1,0:T(8,128)}, f32[512,2048]{1,0:T(8,128)}...) conditional(s32[]{:T(128)} %convert_element_type.258, () %tuple.64, ...), branch_computations={%region_46.47_spmd, %region_47.73_spmd} | conditional | flops 34315198464 | bytes 570207424 | solution.py:566
  603.0 5.4 convolution_convert_fusion.6
  609.9 2.6 copy.269
  615.6 28.2 %while.85 = (s32[]{:T(128)}, bf16[3,512,512]{2,1,0:T(8,128)(2,1)S(1)}, f32[3,8,512,1]{2,1,3,0:T(8,128)S(1)}, bf16[3,512,512]{1,2,0:T(8,128)(2,1)}, pred[3,512,51...) while((s32[]{:T(128)}, ...), condition=%wide.region_53.53_spmd, body=%wide.region_50.52_spmd.sunk | while | flops 562294784 | bytes 33947760 | solution.py:249
  622.3 2.5 fusion.308
  631.7 2.5 fusion.308
  641.1 2.5 fusion.308
  643.9 3.0 fusion.147
  648.5 8.0 multiply_convert_fusion.10
  656.5 4.2 fusion.148
  661.4 5.5 fusion.102
  666.8 5.3 multiply_reduce_fusion.15
  673.8 8.3 multiply_convert_fusion.9
  682.1 8.7 fusion.112
  690.9 4.9 multiply_reduce_fusion.16
  695.8 5.4 fusion.115
  702.9 2.1 fusion.113
  705.0 2.2 convolution_convert_fusion.7
  707.1 70.1 %while.86 = (s32[]{:T(128)}, bf16[3,512,512]{2,1,0:T(8,128)(2,1)}, bf16[3,512,512]{2,1,0:T(8,128)(2,1)}, bf16[3,512,512]{2,1,0:T(8,128)(2,1)}, bf16[3,512,512]{1...) while((s32[]{:T(128)}, bf16[3,512,512]{2,1,0:T(8,128)(2,1)}, ...), condition=%wide.region_64.64_spmd, body=%wide.region_62.63_spmd.sunk | while | flops 1374679040 | bytes 148226256 | solution.py:294
  714.2 2.3 fusion.320
  717.6 5.1 multiply_reduce_fusion.27
  723.5 2.6 multiply_convert_fusion.14
  737.5 2.3 fusion.320
  741.0 5.1 multiply_reduce_fusion.27
  746.8 2.6 multiply_convert_fusion.14
  760.8 2.3 fusion.320
  764.2 5.1 multiply_reduce_fusion.27
  770.1 2.6 multiply_convert_fusion.14
  777.2 7.3 fusion.95
  787.4 3.6 fusion.123
  792.9 3.1 broadcast_add_fusion
  796.5 4.3 add_convert_fusion.20
  800.9 3.6 fusion.120
  804.5 2.4 fusion.122
  806.8 3.0 fusion.121
  809.9 4.1 fusion.119
  818.3 84.7 %shard_map.170 = bf16[512,7296]{1,0:T(8,128)(2,1)} custom-call(bf16[512,7296]{1,0:T(8,128)(2,1)} %pad_dynamic-update-slice_fusion.local), custom_call_target="tpu_custom_call" | custom-call | tf_op jit(solution)/shard_map/pallas_call | solution.py:163
  903.0 4.0 fusion.149
  908.2 6.3 convert_element_type.263
  916.5 2.3 slice_bitcast_fusion.7
  918.7 3.2 slice_bitcast_fusion.6
  921.9 3.8 slice_bitcast_fusion.5
  925.7 4.8 slice_bitcast_fusion.4
  932.9 4.5 add.329
  937.4 2.5 maximum_bitcast_fusion
  (297 shorter events, 129.8 us)
Async XLA Ops:
  1.4 155.6 %copy-start.62 = (f32[3,512]{1,0:T(4,128)}, f32[3,512]{1,0:T(4,128)S(1)}, u32[]{:S(2)}) copy-start(f32[3,512]{1,0:T(4,128)S(1)} %get-tuple-element.924) | copy-start | bytes 18436
  1.4 4.0 copy-start.60
  1.4 5.4 copy-start.5
  5.3 3.5 copy-start.88
  16.1 3.6 copy-start.21
  25.6 5.4 copy-start.22
  31.0 3.6 copy-start.21
  40.4 5.4 copy-start.22
  45.8 3.6 copy-start.21
  55.3 5.4 copy-start.22
  64.8 1.7 copy-start.33
  80.3 1.7 copy-start.47
  87.1 69.9 %collective-permute-start = (bf16[1536,1024]{1,0:T(8,128)(2,1)}, bf16[1536,1024]{1,0:T(8,128)(2,1)S(1)}, u32[]{:S(2)}, u32[]{:S(2)}) collective-permute-start(bf16[1536,1024]{1,0:T(8,128)(2,1)} %get-tuple-element.428), channel_id=1, source_target_pairs={{0,16},{1,17},{2,18},{3,19},{4,20},{5,21},{6,22},{7,23},{8,24},{9,... | collective-permute-start | bytes 9437192 | tf_op jit(solution)/shard_map/ppermute | solution.py:189
  175.8 1.7 copy-start.17
  175.8 5.0 copy-start.70
  175.8 5.0 copy-start.72
  175.8 422.1 %collective-permute-start.1 = (bf16[1536,1024]{1,0:T(8,128)(2,1)}, bf16[1536,1024]{1,0:T(8,128)(2,1)}, u32[]{:S(2)}, u32[]{:S(2)}) collective-permute-start(bf16[1536,1024]{1,0:T(8,128)(2,1)} %get-tuple-element.431), channel_id=1, source_target_pairs={{16,0},{17,1},{18,2},{19,3},{20,4},{21,5},{22,6},{23,7},{24,8},{25... | collective-permute-start | bytes 9437192 | tf_op jit(solution)/shard_map/ppermute | solution.py:189
  177.5 420.4 %copy-start.4 = (bf16[1,3,512,512]{3,2,1,0:T(8,128)(2,1)S(1)}, bf16[1,3,512,512]{3,2,1,0:T(8,128)(2,1)}, u32[]{:S(2)}) copy-start(bf16[1,3,512,512]{3,2,1,0:T(8,128)(2,1)} %param.30) | copy-start | bytes 4718596
  177.5 420.4 %copy-start.59 = (s32[2,3,512]{2,0,1:T(2,128)S(1)}, s32[2,3,512]{2,0,1:T(2,128)}, u32[]{:S(2)}) copy-start(s32[2,3,512]{2,0,1:T(2,128)} %param.31) | copy-start | bytes 36868
  177.5 420.4 %copy-start.63 = (f32[3,512]{1,0:T(4,128)S(1)}, f32[3,512]{1,0:T(4,128)}, u32[]{:S(2)}) copy-start(f32[3,512]{1,0:T(4,128)} %copy-done.62) | copy-start | bytes 18436
  597.9 198.4 %copy-start.73 = (f32[3,512]{1,0:T(4,128)S(1)}, f32[3,512]{1,0:T(4,128)}, u32[]{:S(2)}) copy-start(f32[3,512]{1,0:T(4,128)} %copy-done.72) | copy-start | bytes 18436
  597.9 198.4 %copy-start.71 = (f32[3,512]{1,0:T(4,128)S(1)}, f32[3,512]{1,0:T(4,128)}, u32[]{:S(2)}) copy-start(f32[3,512]{1,0:T(4,128)} %copy-done.70) | copy-start | bytes 18436
  597.9 4.4 copy-start.8
  598.3 4.7 copy-start.53
  599.0 3.9 copy-start.66
  599.1 3.9 copy-start.55
  599.1 3.9 copy-start.68
  603.0 5.4 copy-start.16
  614.0 1.6 copy-start.42
  615.6 28.3 %copy-start.38 = (bf16[512,512]{1,0:T(8,128)(2,1)S(1)}, bf16[512,512]{1,0:T(8,128)(2,1)}, u32[]{:S(2)}) copy-start(bf16[512,512]{1,0:T(8,128)(2,1)} %get-tuple-element.391) | copy-start | bytes 1572868 | tf_op jit(solution)/shard_map/cond
  646.9 1.6 copy-start.85
  648.5 8.0 copy-start.87
  656.5 4.2 copy-start.91
  661.4 5.5 copy-start.50
  702.8 2.1 copy-start.36
  714.2 3.2 copy-start.2
  717.6 5.8 copy-start.3
  737.5 3.2 copy-start.2
  741.0 5.8 copy-start.3
  760.8 3.2 copy-start.2
  764.2 5.8 copy-start.3
  777.2 7.3 copy-start.39
  777.2 7.3 copy-start.40
  777.2 7.3 copy-start.41
  784.5 1.4 copy-start.9
  784.5 2.4 copy-start.37
  784.5 2.4 copy-start.54
  784.5 2.3 copy-start.69
  784.5 2.8 copy-start.90
  787.4 3.6 copy-start.67
  787.4 3.6 copy-start.83
  787.4 3.6 copy-start.56
  790.9 1.9 copy-start.82
  796.5 4.4 copy-start.18
  800.8 3.6 copy-start.45
  804.4 2.4 copy-start.23
  806.8 3.1 copy-start.27
  903.0 5.3 copy-start.13
  925.7 7.2 copy-start.19
  932.9 4.5 copy-start.28
  932.9 4.5 copy-start.29
  932.9 4.5 copy-start.30
  932.9 4.5 copy-start.31
